TPU v7x, 512 devices: a whole 4x4x16 slice. The times are simulated.
512 devices in a mesh: seq: 8 (over y, core), head: 64 (over z, x).
Axes of the slice: x: 4, y: 4, z: 16, core: 2. Of those that a mesh axis runs over, the one named last changes fastest.
Arguments:
- tokens: bfloat16 [8192, 2048], P('seq', 'head'), may hold values from -6 to 6
- z_weight: bfloat16 [2048, 4096], P(None, 'head'), may hold values from -0.125 to 0.125
- x_weight: bfloat16 [2048, 4096], P(None, 'head'), may hold values from -0.79549513 to 0.79549513
- bc_weight: bfloat16 [2048, 256], replicated, may hold values from -0.125 to 0.125
- step_weight: bfloat16 [2048, 64], P(None, 'head'), may hold values from -0.125 to 0.125
- x_kernel: float32 [4, 4096], P(None, 'head'), may hold values from -3 to 3
- bc_kernel: float32 [4, 256], replicated, may hold values from -3 to 3
- step_bias: float32 [64], P('head'), may hold values from -9 to -3
- log_decay: float32 [64], P('head'), may hold values from 0 to 1.5
- skip_gain: float32 [64], P('head'), may hold values from 0.2 to 0.8
- norm_gain: bfloat16 [4096], P('head'), may hold values from 0.099609375 to 1.8984375
- out_weight: bfloat16 [4096, 2048], P('head'), may hold values from -0.09375 to 0.09375
Outputs:
- mixed: bfloat16 [8192, 2048], P('seq', 'head')
All inputs are finite; a program needn't handle non-finite values.
Results may differ from a plain program's by a relative error of at most 0.017.
Values may be sent and summed in bfloat16 or wider, within the bound.
A program may use at most 64 MiB of HBM per device.

v0:
```python
import jax
import jax.numpy as jnp
from jax import lax
from jax.sharding import PartitionSpec as P

CH = 256


def from_behind(block, axis, distance):
    devices = range(lax.axis_size(axis))
    route = [(i - distance, i) for i in devices if i - distance in devices]
    return lax.ppermute(block, axis, route)


def causal(padded, kernel):
    length = padded.shape[0] - 3
    total = kernel[0] * padded[0:length].astype(jnp.float32)
    for offset in range(1, 4):
        total = total + kernel[offset] * padded[offset : offset + length].astype(jnp.float32)
    return jax.nn.silu(total).astype(jnp.bfloat16)


def body(
    tokens,
    z_weight,
    x_weight,
    bc_weight,
    step_weight,
    x_kernel,
    bc_kernel,
    step_bias,
    log_decay,
    skip_gain,
    norm_gain,
    out_weight,
):
    tok_rows = tokens.shape[0]
    heads_here = step_bias.shape[0]
    inner_width = x_weight.shape[1]
    head_size = inner_width // heads_here
    state_size = bc_weight.shape[1] // 2
    piece = lax.all_gather(tokens, "head", axis=1, tiled=True)

    def product(weight):
        return jnp.dot(piece, weight, preferred_element_type=jnp.float32)

    z_sum = product(z_weight)
    x_sum = product(x_weight)
    bc_sum = product(bc_weight)
    step_raw = product(step_weight)
    z_in = z_sum.astype(jnp.bfloat16)
    x_in = x_sum.astype(jnp.bfloat16)
    bc_in = bc_sum.astype(jnp.bfloat16)
    border = jnp.concatenate([x_in[-3:], bc_in[-3:]], axis=1)
    border = from_behind(border, "seq", 1)
    x_conv = causal(jnp.concatenate([border[:, :inner_width], x_in], axis=0), x_kernel)
    bc_conv = causal(jnp.concatenate([border[:, inner_width:], bc_in], axis=0), bc_kernel)
    blocks = tok_rows // CH
    b_map = bc_conv[:, :state_size].reshape(blocks, CH, state_size)
    c_map = bc_conv[:, state_size:].reshape(blocks, CH, state_size)
    step_size = jax.nn.softplus(step_raw + step_bias)
    rate = -jnp.exp(log_decay) * step_size
    values = x_conv.reshape(blocks, CH, heads_here, head_size)
    steps_b = step_size.reshape(blocks, CH, heads_here)
    cumulative = jnp.cumsum(rate.reshape(blocks, CH, heads_here), axis=1)
    lower = (jnp.arange(CH)[:, None] >= jnp.arange(CH)[None, :])[None, :, :, None]
    gram = jnp.einsum("ctn,csn->cts", c_map, b_map, preferred_element_type=jnp.float32)
    spread = cumulative[:, :, None, :] - cumulative[:, None, :, :]
    mixing = jnp.where(
        lower,
        gram[..., None] * jnp.exp(jnp.where(lower, spread, 0.0)) * steps_b[:, None, :, :],
        0.0,
    ).astype(jnp.bfloat16)
    intra = jnp.einsum("ctsh,cshp->cthp", mixing, values, preferred_element_type=jnp.float32)
    tails = jnp.exp(cumulative[:, -1:, :] - cumulative) * steps_b
    weighted = (values.astype(jnp.float32) * tails[..., None]).astype(jnp.bfloat16)
    local = jnp.einsum("cthp,ctn->chpn", weighted, b_map, preferred_element_type=jnp.float32)
    block_decay = jnp.exp(cumulative[:, -1, :])

    def advance(carry, item):
        state, decay = carry
        term, factor = item
        return ((factor[:, None, None] * state + term, decay * factor), (state, decay))

    zero_state = jnp.zeros((heads_here, head_size, state_size), jnp.float32)
    unit_decay = jnp.ones((heads_here,), jnp.float32)
    (shard_state, shard_decay), (local_in, decay_in) = lax.scan(
        advance, (zero_state, unit_decay), (local, block_decay)
    )

    def relay(index, carried):
        return from_behind(shard_decay[:, None, None] * carried + shard_state, "seq", 1)

    incoming = lax.fori_loop(0, lax.axis_size("seq") - 1, relay, zero_state)
    entering = local_in + decay_in[:, :, None, None] * incoming[None]
    held = entering.astype(jnp.bfloat16)
    from_state = (
        jnp.einsum("ctn,chpn->cthp", c_map, held, preferred_element_type=jnp.float32)
        * jnp.exp(cumulative)[..., None]
    )
    output_y = intra + from_state + skip_gain[None, None, :, None] * values.astype(jnp.float32)
    gated = (
        output_y.reshape(tok_rows, inner_width) * jax.nn.silu(z_in.astype(jnp.float32))
    ).astype(jnp.bfloat16)
    head_count = lax.axis_size("head")
    columns = lax.all_to_all(out_weight, "head", split_axis=1, concat_axis=0, tiled=True)
    gain_row = norm_gain.reshape(1, inner_width)
    section = lax.all_gather(gated, "head", axis=1, tiled=True)
    gain_part = lax.all_gather(gain_row, "head", axis=1, tiled=True)
    section_f = section.astype(jnp.float32)
    scaled = (section_f * gain_part.astype(jnp.float32)).astype(jnp.bfloat16)
    partial_out = jnp.dot(scaled, columns, preferred_element_type=jnp.float32)
    squares = jnp.sum(section_f * section_f, axis=1)
    meansq = squares / (inner_width * head_count)
    return (partial_out * lax.rsqrt(meansq + 1e-05)[:, None]).astype(jnp.bfloat16)


def solution(mesh):
    placed = (
        P("seq", "head"),
        P(None, "head"),
        P(None, "head"),
        P(),
        P(None, "head"),
        P(None, "head"),
        P(),
        P("head"),
        P("head"),
        P("head"),
        P("head"),
        P("head", None),
    )
    return jax.shard_map(
        body, mesh=mesh, in_specs=placed, out_specs=P("seq", "head"), check_vma=False
    )
```

profile of v0, /device:TPU:10, one launch (start us, length us, event | category | flops | bytes accessed | tf_op | source)
XLA Modules:
  0.0 403.9 jit_solution(2700277313001061849)
XLA Ops:
  6.5 0.7 all-gather.4.cloned.1.call-update
  9.4 0.8 slice_bitcast_fusion.4
  10.2 0.8 fusion.44
  11.0 148.9 %all-gather.4.cloned.1.call-done = bf16[1024,2048]{0,1:T(8,128)(2,1)} async-done(((bf16[1024,32]{0,1:T(8,128)(2,1)}), bf16[1024,2048]{0,1:T(8,128)(2,1)}) %all-gather.4.cloned.1.call-update) | async-done | bytes 4194320 | tf_op jit(solution)/shard_map/all_gather | solution.py:42
  160.0 2.8 fusion.45
  162.8 1.2 reduce-window.6
  164.1 0.1 copy.67
  164.3 3.6 convolution_convert_fusion
  167.9 0.1 slice.94
  168.0 0.9 convolution_convert_fusion.2
  168.9 0.1 slice.93
  169.0 1.9 collective-permute-start.1
  170.9 0.1 copy.53
  171.2 0.1 exponential_multiply_fusion
  171.3 3.5 collective-permute-done.1
  174.8 1.0 multiply_convert_fusion
  175.8 0.2 copy.68
  176.0 0.2 copy.69
  176.2 0.3 convert_multiply_fusion.2
  176.5 0.1 mul.291
  176.6 0.2 convolution_bitcast_fusion
  176.8 8.1 %while.28 = (s32[]{:T(128)}, f32[1,64,128]{2,1,0:T(8,128)S(1)}, f32[1]{0:T(128)}, f32[4,1,64,128]{3,2,1,0:T(8,128)S(1)}, f32[4,1]{0,1:T(1,128)S(1)}, /*index=5*/...) while((s32[]{:T(128)}, f32[1,64,128]{2,1,0:T(8,128)S(1)}, f32[1]{0:T(128)}, ...), condition=%wide.region_3.4_spmd.clone, body=%wide.region_2.3_spmd.clone.sunk | while | flops 32772 | bytes 164008 | solution.py:87
  176.8 0.6 constant_dynamic-slice_fusion.2
  177.4 0.7 bitcast_add_fusion.4
  178.8 0.6 constant_dynamic-slice_fusion.2
  179.4 0.7 bitcast_add_fusion.4
  180.7 0.1 dynamic_update_slice.14
  180.8 0.6 constant_dynamic-slice_fusion.2
  181.4 0.7 bitcast_add_fusion.4
  182.7 0.1 dynamic_update_slice.14
  182.8 0.6 constant_dynamic-slice_fusion.2
  183.4 0.7 bitcast_add_fusion.4
  184.7 0.1 dynamic_update_slice.14
  184.8 0.5 fusion.10
  185.4 36.8 %while.27 = (s32[]{:T(128)}, f32[1,64,128]{2,1,0:T(8,128)S(1)}, f32[1]{0:T(128)}, f32[1,64,128]{2,1,0:T(8,128)S(1)}, s32[]{:T(128)}) while((s32[]{:T(128)}, f32[1,64,128]{2,1,0:T(8,128)S(1)}, f32[1]{0:T(128)}, f32[1,64,128]{2,1,0:T(8,128)S(1)}, s32[]{:T(128)}) %tuple.53), condition=%wide.region_5.6_spmd, body=%wide.region_4.5_spmd.sunk | while | flops 16386 | bytes 229481 | solution.py:94
  185.4 2.1 collective-permute-start
  187.5 3.3 collective-permute-done
  190.8 1.9 collective-permute-start
  192.7 3.3 collective-permute-done
  196.0 1.9 collective-permute-start
  198.0 3.3 collective-permute-done
  201.3 1.9 collective-permute-start
  203.2 3.3 collective-permute-done
  206.5 1.9 collective-permute-start
  208.4 3.3 collective-permute-done
  211.7 1.9 collective-permute-start
  213.7 3.3 collective-permute-done
  217.0 1.9 collective-permute-start
  218.9 3.3 collective-permute-done
  222.2 0.3 fusion.12
  222.5 0.2 copy.62
  222.7 3.7 multiply_convert_fusion.1
  226.5 0.3 copy.63
  226.8 1.0 reshape.305
  227.8 10.3 %all-to-all-start = ((bf16[64,2,1024]{2,1,0:T(2,128)(2,1)}), bf16[64,2,1024]{2,1,0:T(2,128)(2,1)S(1)}, u32[]{:S(2)}, u32[]{:S(2)}) async-start(bf16[64,2,1024]{2,1,0:T(2,128)(2,1)} %reshape.305), calls=%async_computation | async-start | bytes 524288 | tf_op jit(solution)/shard_map/all_to_all | solution.py:106
  238.1 1.3 dynamic-slice
  240.0 0.2 dynamic-update-slice
  240.3 147.3 %all-reduce = bf16[4096]{0:T(1024)(128)(2,1)S(1)} all-reduce(bf16[4096]{0:T(1024)(128)(2,1)S(1)} %dynamic-update-slice), channel_id=2, replica_groups=mesh['seq'=8,'head'=64] {'head'}, use_global_device_ids=true, to_apply=%add | all-reduce | flops 4096 | bytes 16384
  387.6 0.3 reshape.306
  388.0 0.2 copy.64
  388.2 0.5 all_to_all.17
  388.7 5.2 %fusion.1 = f32[1024]{0:T(1024)S(1)} fusion(bf16[1024,4096]{0,1:T(8,128)(2,1)} %all-gather.6.cloned.1.call-done), kind=kLoop, calls=%fused_computation.7 | loop fusion | flops 12581888 | bytes 8392704 | tf_op jit(solution)/shard_map/reduce_sum | solution.py:113
  394.0 0.5 copy-done.2
  394.5 2.5 fusion.17
  (53 shorter events, 0.7 us)
Async XLA Ops:
  6.5 157.7 %copy-start = (bf16[2048,256]{1,0:T(8,128)(2,1)S(1)}, bf16[2048,256]{1,0:T(8,128)(2,1)}, u32[]{:S(2)}) copy-start(bf16[2048,256]{1,0:T(8,128)(2,1)} %param.19) | copy-start | bytes 3145732
  6.5 153.4 %all-gather.4.cloned.1.call-start = ((), (), s32[]{:S(2)}) async-start(), calls=%async_computation.1 | async-start | bytes 4259840 | tf_op jit(solution)/shard_map/all_gather | solution.py:42
  7.3 381.4 %all-gather.6.cloned.1.call-start = ((), (), s32[]{:S(2)}) async-start(), calls=%async_computation.2 | async-start | bytes 8519680 | tf_op jit(solution)/shard_map/all_gather | solution.py:108
  164.3 3.8 copy-start.1
  164.3 3.8 copy-start.3
  169.0 5.8 %collective-permute-start.1 = (bf16[3,320]{0,1:T(8,128)(2,1)S(1)}, bf16[3,320]{0,1:T(8,128)(2,1)S(1)}, u32[]{:S(2)}, u32[]{:S(2)}) collective-permute-start(bf16[3,320]{0,1:T(8,128)(2,1)S(1)} %pad_maximum_fusion.2), channel_id=1, source_target_pairs={{0,64},{64,128},{128,192},{192,256},{256,320},{320,384},{384,448},... | collective-permute-start | bytes 5768 | tf_op jit(solution)/shard_map/ppermute | solution.py:12
  176.2 46.5 %copy-start.4 = (bf16[2048,64]{0,1:T(8,128)(2,1)S(1)}, bf16[2048,64]{0,1:T(8,128)(2,1)}, u32[]{:S(2)}) copy-start(bf16[2048,64]{0,1:T(8,128)(2,1)} %param.17) | copy-start | bytes 786436
  185.4 41.1 %copy-start.5 = (bf16[64,2048]{1,0:T(8,128)(2,1)S(1)}, bf16[64,2048]{1,0:T(8,128)(2,1)}, u32[]{:S(2)}) copy-start(bf16[64,2048]{1,0:T(8,128)(2,1)} %param.27) | copy-start | bytes 786436
  185.4 5.4 %collective-permute-start = (f32[1,64,128]{2,1,0:T(8,128)S(1)}, f32[1,64,128]{2,1,0:T(8,128)S(1)}, u32[]{:S(2)}, u32[]{:S(2)}) collective-permute-start(f32[1,64,128]{2,1,0:T(8,128)S(1)} %multiply_add_fusion.2), channel_id=1, source_target_pairs={{0,64},{64,128},{128,192},{192,256},{256,320},{320,384},{384,448},... | collective-permute-start | bytes 98312 | tf_op jit(solution)/shard_map/while/body/eval_jaxpr/ppermute | solution.py:12
  190.8 5.2 %collective-permute-start = (f32[1,64,128]{2,1,0:T(8,128)S(1)}, f32[1,64,128]{2,1,0:T(8,128)S(1)}, u32[]{:S(2)}, u32[]{:S(2)}) collective-permute-start(f32[1,64,128]{2,1,0:T(8,128)S(1)} %multiply_add_fusion.2), channel_id=1, source_target_pairs={{0,64},{64,128},{128,192},{192,256},{256,320},{320,384},{384,448},... | collective-permute-start | bytes 98312 | tf_op jit(solution)/shard_map/while/body/eval_jaxpr/ppermute | solution.py:12
  196.0 5.2 %collective-permute-start = (f32[1,64,128]{2,1,0:T(8,128)S(1)}, f32[1,64,128]{2,1,0:T(8,128)S(1)}, u32[]{:S(2)}, u32[]{:S(2)}) collective-permute-start(f32[1,64,128]{2,1,0:T(8,128)S(1)} %multiply_add_fusion.2), channel_id=1, source_target_pairs={{0,64},{64,128},{128,192},{192,256},{256,320},{320,384},{384,448},... | collective-permute-start | bytes 98312 | tf_op jit(solution)/shard_map/while/body/eval_jaxpr/ppermute | solution.py:12
  201.3 5.2 %collective-permute-start = (f32[1,64,128]{2,1,0:T(8,128)S(1)}, f32[1,64,128]{2,1,0:T(8,128)S(1)}, u32[]{:S(2)}, u32[]{:S(2)}) collective-permute-start(f32[1,64,128]{2,1,0:T(8,128)S(1)} %multiply_add_fusion.2), channel_id=1, source_target_pairs={{0,64},{64,128},{128,192},{192,256},{256,320},{320,384},{384,448},... | collective-permute-start | bytes 98312 | tf_op jit(solution)/shard_map/while/body/eval_jaxpr/ppermute | solution.py:12
  206.5 5.2 %collective-permute-start = (f32[1,64,128]{2,1,0:T(8,128)S(1)}, f32[1,64,128]{2,1,0:T(8,128)S(1)}, u32[]{:S(2)}, u32[]{:S(2)}) collective-permute-start(f32[1,64,128]{2,1,0:T(8,128)S(1)} %multiply_add_fusion.2), channel_id=1, source_target_pairs={{0,64},{64,128},{128,192},{192,256},{256,320},{320,384},{384,448},... | collective-permute-start | bytes 98312 | tf_op jit(solution)/shard_map/while/body/eval_jaxpr/ppermute | solution.py:12
  211.7 5.2 %collective-permute-start = (f32[1,64,128]{2,1,0:T(8,128)S(1)}, f32[1,64,128]{2,1,0:T(8,128)S(1)}, u32[]{:S(2)}, u32[]{:S(2)}) collective-permute-start(f32[1,64,128]{2,1,0:T(8,128)S(1)} %multiply_add_fusion.2), channel_id=1, source_target_pairs={{0,64},{64,128},{128,192},{192,256},{256,320},{320,384},{384,448},... | collective-permute-start | bytes 98312 | tf_op jit(solution)/shard_map/while/body/eval_jaxpr/ppermute | solution.py:12
  217.0 5.2 %collective-permute-start = (f32[1,64,128]{2,1,0:T(8,128)S(1)}, f32[1,64,128]{2,1,0:T(8,128)S(1)}, u32[]{:S(2)}, u32[]{:S(2)}) collective-permute-start(f32[1,64,128]{2,1,0:T(8,128)S(1)} %multiply_add_fusion.2), channel_id=1, source_target_pairs={{0,64},{64,128},{128,192},{192,256},{256,320},{320,384},{384,448},... | collective-permute-start | bytes 98312 | tf_op jit(solution)/shard_map/while/body/eval_jaxpr/ppermute | solution.py:12
  222.4 17.6 %copy-start.6 = (bf16[64]{0:T(256)(128)(2,1)S(1)}, bf16[64]{0:T(256)(128)(2,1)}, u32[]{:S(2)}) copy-start(bf16[64]{0:T(256)(128)(2,1)} %param.26) | copy-start | bytes 388
  227.8 159.8 %all-to-all-start = ((bf16[64,2,1024]{2,1,0:T(2,128)(2,1)}), bf16[64,2,1024]{2,1,0:T(2,128)(2,1)S(1)}, u32[]{:S(2)}, u32[]{:S(2)}) async-start(bf16[64,2,1024]{2,1,0:T(2,128)(2,1)} %reshape.305), calls=%async_computation | async-start | bytes 524288 | tf_op jit(solution)/shard_map/all_to_all | solution.py:106
  388.7 5.8 %copy-start.2 = (bf16[1024,4096]{0,1:T(8,128)(2,1)S(1)}, bf16[1024,4096]{0,1:T(8,128)(2,1)}, u32[]{:S(2)}) copy-start(bf16[1024,4096]{0,1:T(8,128)(2,1)} %all-gather.6.cloned.1.call-done) | copy-start | bytes 25165828
Sparse Core Ops, SparseCore 0:
  10.3 149.6 all-gather.3
  226.6 154.3 all-gather.5
where the time goes:
time: 404 us
  waiting for transfers between devices  176 us (44%)
  blocking collectives  147 us (36%)
  starting transfers between devices  25.8 us (6%)
  between operations  16.4 us (4%)
  matrix products  14.6 us (4%)
  other arithmetic  10.6 us (3%)
  local copies, waits for them, and re-layouts  10.1 us (2%)
    all_gather x1, waiting for transfers between devices, body(): piece = lax.all_gather(tokens, 'head', axis=1, tiled=True)  149 us
    unnamed x1, blocking collectives  147 us
    ppermute x8, waiting for transfers between devices, from_behind(): return lax.ppermute(block, axis, route)  26.6 us
    ppermute x8, starting transfers between devices, from_behind(): return lax.ppermute(block, axis, route)  15.4 us
    dot_general x4, matrix products, product(): return jnp.dot(piece, weight, preferred_element_type=jnp.float32)  11.1 us
    all_to_all x1, starting transfers between devices, body(): lax.all_to_all(out_weight, 'head', split_axis=1, concat_axis=0, tiled=True)  10.3 us
  transfers between devices with their start and end apart: 11, of which 9 were waited for; matrix products, arithmetic and copies ran while one was open for 1% of the time, Pallas kernels for 0%

commit v1 on v0

--- a/solution.py
+++ b/solution.py
@@ -103,7 +103,9 @@
         output_y.reshape(tok_rows, inner_width) * jax.nn.silu(z_in.astype(jnp.float32))
     ).astype(jnp.bfloat16)
     head_count = lax.axis_size("head")
-    columns = lax.all_to_all(out_weight, "head", split_axis=1, concat_axis=0, tiled=True)
+    pieces = jnp.split(out_weight, lax.axis_size("head"), axis=1)
+    received = lax.all_to_all(jnp.stack(pieces), "head", 0, 0)
+    columns = jnp.concatenate(received, axis=0)
     gain_row = norm_gain.reshape(1, inner_width)
     section = lax.all_gather(gated, "head", axis=1, tiled=True)
     gain_part = lax.all_gather(gain_row, "head", axis=1, tiled=True)

time: 404 us -> 412 us (1.020)
  local copies, waits for them, and re-layouts: 10.1 us -> 16.6 us
    unnamed x21 -> x147, local copies, waits for them, and re-layouts: 3.76 us -> 9.74 us
  transfers between devices with their start and end apart: 11 -> 11, of which waited for: 9 -> 9; matrix products, arithmetic and copies ran while one was open for 1% -> 3% of each run, Pallas kernels for 0% -> 0%
where the time goes in v1:
time: 412 us; the launch traced here: 411 us
  waiting for transfers between devices  177 us (43%)
  blocking collectives  148 us (36%)
  starting transfers between devices  25.7 us (6%)
  local copies, waits for them, and re-layouts  16.6 us (4%)
  between operations  16.6 us (4%)
  matrix products  14.5 us (4%)
  other arithmetic  10.7 us (3%)
    all_gather x1, waiting for transfers between devices, body(): piece = lax.all_gather(tokens, 'head', axis=1, tiled=True)  149 us
    unnamed x1, blocking collectives  148 us
    ppermute x8, waiting for transfers between devices, from_behind(): return lax.ppermute(block, axis, route)  26.8 us
    ppermute x8, starting transfers between devices, from_behind(): return lax.ppermute(block, axis, route)  15.4 us
    dot_general x4, matrix products, product(): return jnp.dot(piece, weight, preferred_element_type=jnp.float32)  11 us
    all_to_all x1, starting transfers between devices, body(): received = lax.all_to_all(jnp.stack(pieces), 'head', 0, 0)  10.3 us
    unnamed x147, local copies, waits for them, and re-layouts  9.74 us
  transfers between devices with their start and end apart: 11, of which 9 were waited for; matrix products, arithmetic and copies ran while one was open for 3% of the time, Pallas kernels for 0%

profile of v1, /device:TPU:10, one launch (start us, length us, event | category | flops | bytes accessed | tf_op | source)
XLA Modules:
  0.0 411.1 jit_solution(3887858993039383165)
XLA Ops:
  6.5 0.7 all-gather.4.cloned.1.call-update
  9.4 0.8 slice_bitcast_fusion.4
  10.2 0.8 fusion.48
  11.0 148.9 %all-gather.4.cloned.1.call-done = bf16[1024,2048]{0,1:T(8,128)(2,1)} async-done(((bf16[1024,32]{0,1:T(8,128)(2,1)}), bf16[1024,2048]{0,1:T(8,128)(2,1)}) %all-gather.4.cloned.1.call-update) | async-done | bytes 4194320 | tf_op jit(solution)/shard_map/all_gather | solution.py:42
  160.0 2.8 fusion.49
  162.8 1.2 reduce-window.6
  164.1 0.1 copy.255
  164.3 0.1 copy.178
  164.5 3.6 convolution_convert_fusion
  168.3 0.9 convolution_convert_fusion.2
  169.2 1.9 collective-permute-start.1
  171.3 3.7 collective-permute-done.1
  175.0 1.0 multiply_convert_fusion
  176.1 0.2 copy.257
  176.3 0.3 convert_multiply_fusion.2
  176.6 0.2 convolution_bitcast_fusion
  176.8 8.1 %while.28 = (s32[]{:T(128)}, f32[1,64,128]{2,1,0:T(8,128)S(1)}, f32[1]{0:T(128)}, f32[4,1,64,128]{3,2,1,0:T(8,128)S(1)}, f32[4,1]{0,1:T(1,128)S(1)}, /*index=5*/...) while((s32[]{:T(128)}, f32[1,64,128]{2,1,0:T(8,128)S(1)}, f32[1]{0:T(128)}, ...), condition=%wide.region_3.4_spmd.clone, body=%wide.region_2.3_spmd.clone.sunk | while | flops 32772 | bytes 164000 | solution.py:87
  176.8 0.6 constant_dynamic-slice_fusion.2
  177.4 0.7 bitcast_add_fusion.4
  178.8 0.6 constant_dynamic-slice_fusion.2
  179.4 0.7 bitcast_add_fusion.4
  180.7 0.1 dynamic_update_slice.14
  180.8 0.6 constant_dynamic-slice_fusion.2
  181.4 0.7 bitcast_add_fusion.4
  182.7 0.1 dynamic_update_slice.14
  182.8 0.6 constant_dynamic-slice_fusion.2
  183.4 0.7 bitcast_add_fusion.4
  184.7 0.1 dynamic_update_slice.14
  184.8 0.2 copy.256
  185.0 0.1 mul.291
  185.1 0.5 fusion.10
  185.7 36.8 %while.27 = (s32[]{:T(128)}, f32[1,64,128]{2,1,0:T(8,128)S(1)}, f32[1]{0:T(128)}, f32[1,64,128]{2,1,0:T(8,128)S(1)}, s32[]{:T(128)}) while((s32[]{:T(128)}, f32[1,64,128]{2,1,0:T(8,128)S(1)}, f32[1]{0:T(128)}, f32[1,64,128]{2,1,0:T(8,128)S(1)}, s32[]{:T(128)}) %tuple.113), condition=%wide.region_5.6_spmd, body=%wide.region_4.5_spmd.sunk | while | flops 16386 | bytes 229481 | solution.py:94
  185.7 2.1 collective-permute-start
  187.8 3.3 collective-permute-done
  191.1 1.9 collective-permute-start
  193.0 3.3 collective-permute-done
  196.3 1.9 collective-permute-start
  198.3 3.3 collective-permute-done
  201.6 1.9 collective-permute-start
  203.5 3.3 collective-permute-done
  206.8 1.9 collective-permute-start
  208.7 3.3 collective-permute-done
  212.0 1.9 collective-permute-start
  214.0 3.3 collective-permute-done
  217.3 1.9 collective-permute-start
  219.2 3.3 collective-permute-done
  222.5 0.3 fusion.12
  222.7 0.2 copy.187
  223.0 3.7 multiply_convert_fusion.1
  226.7 0.1 fusion.47
  227.5 0.2 fusion.46
  229.3 0.2 fusion.45
  231.2 0.2 fusion.44
  233.8 1.0 reshape.306
  234.9 10.3 %all-to-all-start = ((bf16[64,2,1024]{2,1,0:T(2,128)(2,1)}), bf16[64,2,1024]{2,1,0:T(2,128)(2,1)S(1)}, u32[]{:S(2)}, u32[]{:S(2)}) async-start(bf16[64,2,1024]{2,1,0:T(2,128)(2,1)} %reshape.306), calls=%async_computation | async-start | bytes 524288 | tf_op jit(solution)/shard_map/all_to_all | solution.py:107
  245.1 1.3 dynamic-slice
  247.1 0.2 dynamic-update-slice
  247.3 147.6 %all-reduce = bf16[4096]{0:T(1024)(128)(2,1)S(1)} all-reduce(bf16[4096]{0:T(1024)(128)(2,1)S(1)} %dynamic-update-slice), channel_id=2, replica_groups=mesh['seq'=8,'head'=64] {'head'}, use_global_device_ids=true, to_apply=%add | all-reduce | flops 4096 | bytes 16384
  394.9 0.3 reshape.307
  395.3 0.2 copy.252
  395.5 0.5 reshape.293
  396.0 5.2 %fusion.1 = f32[1024]{0:T(1024)S(1)} fusion(bf16[1024,4096]{0,1:T(8,128)(2,1)} %all-gather.6.cloned.1.call-done), kind=kLoop, calls=%fused_computation.7 | loop fusion | flops 12581888 | bytes 8392704 | tf_op jit(solution)/shard_map/reduce_sum | solution.py:115
  401.2 0.5 copy-done.2
  401.7 2.5 fusion.17
  (183 shorter events, 7.2 us)
Async XLA Ops:
  6.5 158.0 %copy-start = (bf16[2048,256]{1,0:T(8,128)(2,1)S(1)}, bf16[2048,256]{1,0:T(8,128)(2,1)}, u32[]{:S(2)}) copy-start(bf16[2048,256]{1,0:T(8,128)(2,1)} %param.19) | copy-start | bytes 3145732
  6.5 153.4 %all-gather.4.cloned.1.call-start = ((), (), s32[]{:S(2)}) async-start(), calls=%async_computation.1 | async-start | bytes 4259840 | tf_op jit(solution)/shard_map/all_gather | solution.py:42
  7.3 388.7 %all-gather.6.cloned.1.call-start = ((), (), s32[]{:S(2)}) async-start(), calls=%async_computation.2 | async-start | bytes 8519680 | tf_op jit(solution)/shard_map/all_gather | solution.py:110
  164.5 3.8 copy-start.1
  164.5 3.8 copy-start.4
  169.2 5.8 %collective-permute-start.1 = (bf16[3,320]{0,1:T(8,128)(2,1)S(1)}, bf16[3,320]{0,1:T(8,128)(2,1)S(1)}, u32[]{:S(2)}, u32[]{:S(2)}) collective-permute-start(bf16[3,320]{0,1:T(8,128)(2,1)S(1)} %pad_maximum_fusion.2), channel_id=1, source_target_pairs={{0,64},{64,128},{128,192},{192,256},{256,320},{320,384},{384,448},... | collective-permute-start | bytes 5768 | tf_op jit(solution)/shard_map/ppermute | solution.py:12
  176.6 46.4 %copy-start.5 = (bf16[2048,64]{0,1:T(8,128)(2,1)S(1)}, bf16[2048,64]{0,1:T(8,128)(2,1)}, u32[]{:S(2)}) copy-start(bf16[2048,64]{0,1:T(8,128)(2,1)} %param.17) | copy-start | bytes 786436
  185.7 41.0 %copy-start.3 = (bf16[64,2048]{1,0:T(8,128)(2,1)S(1)}, bf16[64,2048]{1,0:T(8,128)(2,1)}, u32[]{:S(2)}) copy-start(bf16[64,2048]{1,0:T(8,128)(2,1)} %param.27) | copy-start | bytes 786436
  185.7 5.4 %collective-permute-start = (f32[1,64,128]{2,1,0:T(8,128)S(1)}, f32[1,64,128]{2,1,0:T(8,128)S(1)}, u32[]{:S(2)}, u32[]{:S(2)}) collective-permute-start(f32[1,64,128]{2,1,0:T(8,128)S(1)} %multiply_add_fusion.2), channel_id=1, source_target_pairs={{0,64},{64,128},{128,192},{192,256},{256,320},{320,384},{384,448},... | collective-permute-start | bytes 98312 | tf_op jit(solution)/shard_map/while/body/eval_jaxpr/ppermute | solution.py:12
  191.1 5.2 %collective-permute-start = (f32[1,64,128]{2,1,0:T(8,128)S(1)}, f32[1,64,128]{2,1,0:T(8,128)S(1)}, u32[]{:S(2)}, u32[]{:S(2)}) collective-permute-start(f32[1,64,128]{2,1,0:T(8,128)S(1)} %multiply_add_fusion.2), channel_id=1, source_target_pairs={{0,64},{64,128},{128,192},{192,256},{256,320},{320,384},{384,448},... | collective-permute-start | bytes 98312 | tf_op jit(solution)/shard_map/while/body/eval_jaxpr/ppermute | solution.py:12
  196.3 5.2 %collective-permute-start = (f32[1,64,128]{2,1,0:T(8,128)S(1)}, f32[1,64,128]{2,1,0:T(8,128)S(1)}, u32[]{:S(2)}, u32[]{:S(2)}) collective-permute-start(f32[1,64,128]{2,1,0:T(8,128)S(1)} %multiply_add_fusion.2), channel_id=1, source_target_pairs={{0,64},{64,128},{128,192},{192,256},{256,320},{320,384},{384,448},... | collective-permute-start | bytes 98312 | tf_op jit(solution)/shard_map/while/body/eval_jaxpr/ppermute | solution.py:12
  201.6 5.2 %collective-permute-start = (f32[1,64,128]{2,1,0:T(8,128)S(1)}, f32[1,64,128]{2,1,0:T(8,128)S(1)}, u32[]{:S(2)}, u32[]{:S(2)}) collective-permute-start(f32[1,64,128]{2,1,0:T(8,128)S(1)} %multiply_add_fusion.2), channel_id=1, source_target_pairs={{0,64},{64,128},{128,192},{192,256},{256,320},{320,384},{384,448},... | collective-permute-start | bytes 98312 | tf_op jit(solution)/shard_map/while/body/eval_jaxpr/ppermute | solution.py:12
  206.8 5.2 %collective-permute-start = (f32[1,64,128]{2,1,0:T(8,128)S(1)}, f32[1,64,128]{2,1,0:T(8,128)S(1)}, u32[]{:S(2)}, u32[]{:S(2)}) collective-permute-start(f32[1,64,128]{2,1,0:T(8,128)S(1)} %multiply_add_fusion.2), channel_id=1, source_target_pairs={{0,64},{64,128},{128,192},{192,256},{256,320},{320,384},{384,448},... | collective-permute-start | bytes 98312 | tf_op jit(solution)/shard_map/while/body/eval_jaxpr/ppermute | solution.py:12
  212.0 5.2 %collective-permute-start = (f32[1,64,128]{2,1,0:T(8,128)S(1)}, f32[1,64,128]{2,1,0:T(8,128)S(1)}, u32[]{:S(2)}, u32[]{:S(2)}) collective-permute-start(f32[1,64,128]{2,1,0:T(8,128)S(1)} %multiply_add_fusion.2), channel_id=1, source_target_pairs={{0,64},{64,128},{128,192},{192,256},{256,320},{320,384},{384,448},... | collective-permute-start | bytes 98312 | tf_op jit(solution)/shard_map/while/body/eval_jaxpr/ppermute | solution.py:12
  217.3 5.2 %collective-permute-start = (f32[1,64,128]{2,1,0:T(8,128)S(1)}, f32[1,64,128]{2,1,0:T(8,128)S(1)}, u32[]{:S(2)}, u32[]{:S(2)}) collective-permute-start(f32[1,64,128]{2,1,0:T(8,128)S(1)} %multiply_add_fusion.2), channel_id=1, source_target_pairs={{0,64},{64,128},{128,192},{192,256},{256,320},{320,384},{384,448},... | collective-permute-start | bytes 98312 | tf_op jit(solution)/shard_map/while/body/eval_jaxpr/ppermute | solution.py:12
  226.7 20.4 %copy-start.6 = (bf16[64]{0:T(256)(128)(2,1)S(1)}, bf16[64]{0:T(256)(128)(2,1)}, u32[]{:S(2)}) copy-start(bf16[64]{0:T(256)(128)(2,1)} %param.26) | copy-start | bytes 388
  234.9 160.1 %all-to-all-start = ((bf16[64,2,1024]{2,1,0:T(2,128)(2,1)}), bf16[64,2,1024]{2,1,0:T(2,128)(2,1)S(1)}, u32[]{:S(2)}, u32[]{:S(2)}) async-start(bf16[64,2,1024]{2,1,0:T(2,128)(2,1)} %reshape.306), calls=%async_computation | async-start | bytes 524288 | tf_op jit(solution)/shard_map/all_to_all | solution.py:107
  396.0 5.8 %copy-start.2 = (bf16[1024,4096]{0,1:T(8,128)(2,1)S(1)}, bf16[1024,4096]{0,1:T(8,128)(2,1)}, u32[]{:S(2)}) copy-start(bf16[1024,4096]{0,1:T(8,128)(2,1)} %all-gather.6.cloned.1.call-done) | copy-start | bytes 25165828
Sparse Core Ops, SparseCore 0:
  10.3 149.6 all-gather.3
  226.9 155.2 all-gather.5
